TPU v7x, 32 devices: a whole 2x2x4 slice. The times are simulated.
32 devices in a mesh: tm: 8 (over y, x, core), user: 4 (over z).
Axes of the slice: x: 2, y: 2, z: 4, core: 2. Of those that a mesh axis runs over, the one named last changes fastest.
Arguments:
- events: bfloat16 [4, 8192, 512], P('user', 'tm'), may hold values from -6 to 6
- w_first: bfloat16 [512, 1024], replicated, may hold values from -0.25 to 0.25
- b_first: float32 [1024], replicated, may hold values from -3 to 3
- w_second: bfloat16 [1024, 512], replicated, may hold values from -0.1875 to 0.1875
- count_embed: float32 [512], replicated, may hold values from -0.3 to 0.3
- norm_gain: float32 [512], replicated, may hold values from 0.5 to 1.5
- event_session: int32 [4, 8192], P('user', 'tm'), may hold values from 0 to 511, as said below
- event_count: int32 [4, 8], P('user', 'tm'), may hold values from 256 to 1024, as said below
- session_user: int32 [4, 512], P('user', 'tm'), may hold values from 0 to 65535, as said below
Outputs:
- section_rows: bfloat16 [8, 4, 128, 512], P('tm', 'user')
- section_users: int32 [8, 4, 128], P('tm', 'user')
Inputs may be any that keep to these rules, and one draw needn't show every extreme that they name: `event_session`: the events of time slice t (slots t * 1024 to (t + 1) * 1024 - 1 of a shard) name sessions of slices max(0, t - 4) to t only; some sessions have no valid event. `event_count`: some time slice of some shard has all 1024 events valid. `session_user`: among the 64 sessions of one shard and time slice, at most 32 have users of the same section (user mod 4); in every time slice some section gets exactly 32 from every shard.
All inputs are finite; a program needn't handle non-finite values.
Results may differ from a plain program's by a relative error of at most 0.0042.
Values may be sent and summed in bfloat16 or wider, within the bound.
A program may use at most 64 MiB of HBM per device.

v0:
```python
import functools
import math

import jax
import jax.numpy as jnp
from jax import lax
from jax.experimental import pallas as pl
from jax.experimental.pallas import tpu as pltpu
from jax.sharding import PartitionSpec as P

MESH = pl.DeviceIdType.MESH
BF16 = jnp.bfloat16
F32 = jnp.float32
I32 = jnp.int32
VMEM_BYTES = 63 << 20


def iota(shape, axis):
    return lax.broadcasted_iota(I32, shape, axis)


def kernel(
    n_tm,
    n_sec,
    reach,
    cap,
    events,
    w_first,
    w_second,
    b_first,
    count_embed,
    norm_gain,
    event_session,
    event_count,
    session_user,
    out_rows,
    out_users,
    ev_v,
    w1_v,
    w2_v,
    b1_v,
    embed_v,
    gain_v,
    ids_v,
    count_v,
    user_v,
    acc,
    cnt_send,
    cnt_recv,
    sums_send,
    sums_recv,
    rows_send,
    rows_recv,
    users_send,
    users_recv,
    small_sem,
    ev_sem,
    w1_sem,
    w2_sem,
    sums_ss,
    sums_rs,
    cnt_ss,
    cnt_rs,
    rows_ss,
    rows_rs,
    users_ss,
    users_rs,
):
    t = lax.axis_index("tm")
    u = lax.axis_index("user")
    ev_rows, width = ev_v.shape
    hidden = w1_v.shape[1]
    sess = user_v.shape[1]
    held = (reach + 1) * sess
    step = min(256, hidden)
    parts = hidden // step

    def load(src, dst, sem):
        copy = pltpu.make_async_copy(src, dst, sem)
        copy.start()
        return copy

    small = [
        load(src, dst, small_sem.at[i])
        for i, (src, dst) in enumerate(
            (
                (event_session, ids_v),
                (event_count, count_v),
                (session_user, user_v),
                (b_first, b1_v),
                (count_embed, embed_v),
                (norm_gain, gain_v),
            )
        )
    ]
    w1_load, w2_load = [], []
    for i in range(parts):
        cols = pl.ds(i * step, step)
        w1_load.append(load(w_first.at[:, cols], w1_v.at[:, cols], w1_sem.at[i]))
        if i == 0:
            ev_load = load(events.at[0], ev_v, ev_sem)
    for i in range(parts):
        cols = pl.ds(i * step, step)
        w2_load.append(load(w_second.at[cols], w2_v.at[cols], w2_sem.at[i]))

    barrier = pltpu.get_barrier_semaphore()

    def greet(device):
        pl.semaphore_signal(barrier, inc=1, device_id=device, device_id_type=MESH)

    for d in range(1, reach + 1):

        @pl.when(t + d < n_tm)
        def _(d=d):
            greet({"tm": t + d})

    for k in range(1, n_sec):
        greet({"user": lax.rem(u + k, n_sec)})

    def sums_copy(d):
        return pltpu.make_async_remote_copy(
            src_ref=sums_send.at[reach - d],
            dst_ref=sums_recv.at[d - 1],
            send_sem=sums_ss.at[d - 1],
            recv_sem=sums_rs.at[d - 1],
            device_id={"tm": t - d},
            device_id_type=MESH,
        )

    def cnt_copy(d):
        return pltpu.make_async_remote_copy(
            src_ref=cnt_send.at[d],
            dst_ref=cnt_recv.at[d - 1],
            send_sem=cnt_ss.at[d - 1],
            recv_sem=cnt_rs.at[d - 1],
            device_id={"tm": t - d},
            device_id_type=MESH,
        )

    def routed_copy(k, send, recv, ss, rs):
        v = lax.rem(u + k, n_sec)
        return pltpu.make_async_remote_copy(
            src_ref=send.at[v],
            dst_ref=recv.at[u],
            send_sem=ss.at[k - 1],
            recv_sem=rs.at[k - 1],
            device_id={"user": v},
            device_id_type=MESH,
        )

    def rows_copy(k):
        return routed_copy(k, rows_send, rows_recv, rows_ss, rows_rs)

    def users_copy(k):
        return routed_copy(k, users_send, users_recv, users_ss, users_rs)

    c_one = math.sqrt(2.0 / math.pi)
    c_three = c_one * 0.044715

    def activated(i):
        cols = slice(i * step, (i + 1) * step)
        tiles = []
        for first in range(0, ev_rows, 256):
            x = jnp.dot(
                ev_v[first : first + 256],
                w1_v[:, cols],
                preferred_element_type=F32,
            )
            x = x + b1_v[:, cols]
            twice = x + x * jnp.tanh(x * (c_one + c_three * (x * x)))
            tiles.append(twice.astype(BF16))
        return jnp.concatenate(tiles, axis=0)

    def second_product(i, active, rows):
        cols = slice(i * step, (i + 1) * step)
        pooled = jnp.dot(assign[rows], active, preferred_element_type=F32)
        return jnp.dot(pooled.astype(BF16), w2_v[cols, :], preferred_element_type=F32)

    for copy in small:
        copy.wait()
    w1_load[0].wait()
    ev_load.wait()
    active = activated(0)

    ids = ids_v[...]
    local = ids - (t - reach) * sess
    lane = iota((1, ev_rows), 1)
    local = jnp.where(lane < count_v[...], local, -1)
    belongs = jnp.where(local == iota((held, ev_rows), 0), 1.0, 0.0)
    assign = belongs.astype(BF16)

    for copy in w1_load[1:] + w2_load:
        copy.wait()
    far = (reach + 1) // 2 * sess
    total = second_product(0, active, slice(0, held))
    for i in range(1, parts - 1):
        total = total + second_product(i, activated(i), slice(0, held))
    active = activated(parts - 1)
    first_half = total[:far] + second_product(parts - 1, active, slice(0, far))
    sums_send[: far // sess] = first_half.reshape(-1, sess, width).astype(BF16)

    pl.semaphore_wait(barrier, jnp.minimum(t, reach) + n_sec - 1)

    def send_sums(d):
        @pl.when(t >= d)
        def _():
            sums_copy(d).start()

    for d in range(reach, reach - far // sess, -1):
        send_sums(d)
    rest = total[far:] + second_product(parts - 1, active, slice(far, held))
    near = rest[: held - far - sess]
    sums_send[far // sess :] = near.reshape(-1, sess, width).astype(BF16)
    for d in range(reach - far // sess, 0, -1):
        send_sums(d)
    acc[...] = rest[held - far - sess :]

    totals = jnp.sum(belongs, axis=1, keepdims=True)
    diagonal = iota((sess, 128), 0) == iota((sess, 128), 1)
    for d in range(reach + 1):
        first = (reach - d) * sess
        as_row = jnp.where(diagonal, totals[first : first + sess], 0.0)
        cnt_send[d] = jnp.broadcast_to(
            jnp.sum(as_row, axis=0, keepdims=True), (8, 128)
        )
    for d in range(reach, 0, -1):

        @pl.when(t >= d)
        def _(d=d):
            cnt_copy(d).start()

    user_row = user_v[...]
    square = iota((sess, sess), 0), iota((sess, sess), 1)
    user_col = jnp.sum(
        jnp.where(square[0] == square[1], user_row, 0), axis=1, keepdims=True
    )
    sec_row = lax.rem(user_row, n_sec)
    sec_col = lax.rem(user_col, n_sec)
    same = jnp.where(sec_row == sec_col, 1, 0)
    rank_row = jnp.sum(
        jnp.where(square[0] < square[1], same, 0), axis=0, keepdims=True
    )
    rank_col = jnp.sum(
        jnp.where(square[1] < square[0], same, 0), axis=1, keepdims=True
    )
    padded = rows_send.shape[1]
    place = jnp.where(
        sec_row * padded + rank_row == iota((n_sec * padded, sess), 0), 1.0, 0.0
    ).astype(BF16)
    slots = n_sec * cap
    at = iota((sess, slots), 1) == rank_col + u * cap
    for v in range(n_sec):
        named = jnp.where(at & (sec_col == v), user_col + 1, 0)
        users_send[v] = jnp.broadcast_to(
            jnp.sum(named, axis=0, keepdims=True), (8, slots)
        )
    for k in range(1, n_sec):
        users_copy(k).start()
    users_recv[u] = users_send[u]

    for d in range(1, reach + 1):

        @pl.when(t + d < n_tm)
        def _(d=d):
            cnt_copy(d).wait_recv()
            cnt_send[0] += cnt_recv[d - 1]

    count = jnp.sum(
        jnp.where(diagonal, cnt_send[0][:1], 0.0), axis=1, keepdims=True
    )
    share = 0.5 / jnp.maximum(count, 1.0)
    embedded = jnp.log(1.0 + count) * embed_v[...]
    for k in range(1, n_sec):
        users_copy(k).wait_recv()
    out_users[0] = jnp.sum(users_recv[...], axis=0)[:1] - 1

    for d in range(1, reach + 1):

        @pl.when(t + d < n_tm)
        def _(d=d):
            sums_copy(d).wait_recv()
            acc[...] += sums_recv[d - 1].astype(F32)

    mixed = acc[...] * share + embedded
    mean = jnp.mean(mixed * mixed, axis=1, keepdims=True)
    rows = (mixed * lax.rsqrt(mean + 1e-06) * gain_v[...]).astype(BF16)
    outgoing = jnp.dot(place, rows, preferred_element_type=F32).astype(BF16)
    rows_send[...] = outgoing.reshape(n_sec, padded, width)
    for k in range(1, n_sec):
        rows_copy(k).start()
    rows_recv[u] = rows_send[u]

    for d in range(1, reach + 1):

        @pl.when(t >= d)
        def _(d=d):
            cnt_copy(d).wait_send()
            sums_copy(d).wait_send()

    for k in range(1, n_sec):
        users_copy(k).wait_send()
        rows_copy(k).wait_send()
    for k in range(1, n_sec):
        rows_copy(k).wait_recv()
    if padded == cap:
        out_rows[0, 0] = rows_recv[...].reshape(slots, width)
    else:
        whole = rows_recv[...].astype(F32)[:, :cap]
        out_rows[0, 0] = whole.reshape(slots, width).astype(BF16)


def on_device(
    n_tm,
    n_sec,
    events,
    w_first,
    b_first,
    w_second,
    count_embed,
    norm_gain,
    event_session,
    event_count,
    session_user,
):
    _, ev_rows, width = events.shape
    hidden = w_first.shape[1]
    sess = session_user.shape[1]
    reach = n_tm // 2
    cap = max(2, 2 * sess // n_sec)
    padded = -(-cap // 16) * 16
    slots = n_sec * cap
    parts = hidden // min(256, hidden)
    dma = pltpu.SemaphoreType.DMA
    vmem = pl.BlockSpec(memory_space=pltpu.VMEM)
    hbm = pl.BlockSpec(memory_space=pl.ANY)
    return pl.pallas_call(
        functools.partial(kernel, n_tm, n_sec, reach, cap),
        out_shape=(
            jax.ShapeDtypeStruct((1, 1, slots, width), BF16),
            jax.ShapeDtypeStruct((1, 1, slots), I32),
        ),
        in_specs=[hbm] * 9,
        out_specs=(vmem, vmem),
        scratch_shapes=[
            pltpu.VMEM((ev_rows, width), BF16),
            pltpu.VMEM((width, hidden), BF16),
            pltpu.VMEM((hidden, width), BF16),
            pltpu.VMEM((1, hidden), F32),
            pltpu.VMEM((1, width), F32),
            pltpu.VMEM((1, width), F32),
            pltpu.VMEM((1, ev_rows), I32),
            pltpu.VMEM((1, 1), I32),
            pltpu.VMEM((1, sess), I32),
            pltpu.VMEM((sess, width), F32),
            pltpu.VMEM((reach + 1, 8, 128), F32),
            pltpu.VMEM((reach, 8, 128), F32),
            pltpu.VMEM((reach, sess, width), BF16),
            pltpu.VMEM((reach, sess, width), BF16),
            pltpu.VMEM((n_sec, padded, width), BF16),
            pltpu.VMEM((n_sec, padded, width), BF16),
            pltpu.VMEM((n_sec, 8, slots), I32),
            pltpu.VMEM((n_sec, 8, slots), I32),
            dma((6,)),
            dma,
            dma((parts,)),
            dma((parts,)),
            dma((reach,)),
            dma((reach,)),
            dma((reach,)),
            dma((reach,)),
            dma((n_sec - 1,)),
            dma((n_sec - 1,)),
            dma((n_sec - 1,)),
            dma((n_sec - 1,)),
        ],
        compiler_params=pltpu.CompilerParams(
            collective_id=0, has_side_effects=True, vmem_limit_bytes=VMEM_BYTES
        ),
        name="pool_and_route",
    )(
        events,
        w_first,
        w_second,
        b_first.reshape(1, hidden),
        count_embed.reshape(1, width),
        norm_gain.reshape(1, width),
        event_session,
        event_count,
        session_user,
    )


def solution(mesh):
    in_specs = (
        P("user", "tm", None),
        P(),
        P(),
        P(),
        P(),
        P(),
        P("user", "tm"),
        P("user", "tm"),
        P("user", "tm"),
    )
    out_specs = (P("tm", "user", None, None), P("tm", "user", None))
    return jax.shard_map(
        functools.partial(on_device, mesh.shape["tm"], mesh.shape["user"]),
        mesh=mesh,
        in_specs=in_specs,
        out_specs=out_specs,
        check_vma=False,
    )
```

profile of v0, /device:TPU:2, one launch (start us, length us, event | category | flops | bytes accessed | tf_op | source)
XLA Modules:
  0.0 23.4 jit_solution(9217572225141991927)
XLA Ops:
  1.3 20.1 %pool_and_route.1 = (bf16[1,1,128,512]{3,2,1,0:T(8,128)(2,1)}, s32[1,1,128]{2,1,0:T(1,128)}) custom-call(bf16[1,1024,512]{2,1,0:T(8,128)(2,1)} %events.1, bf16[512,1024]{1,0:T(8,128)(2,1)} %w_first.1, bf16[1024,512]{1,0:T(8,128)(2,1)} %w_second.1, f32[1,1024]{1,0:T(1,128)} %bitcast.3, f32[1,512]{1,0:T(1,128)} %bitcast.4, f32[1,512]{1,0:T(1,128)} %bitcast.5, ...), custom_call_target="tpu_custom_call" | custom-call | tf_op jit(solution)/shard_map/pool_and_route/pallas_call | solution.py:336
  21.3 0.0 copy-start
  21.4 1.6 %copy.14 = bf16[1,1,128,512]{3,2,1,0:T(8,128)(2,1)} copy(bf16[1,1,128,512]{3,2,1,0:T(8,128)(2,1)} %get-tuple-element.4) | data formatting | bytes 262144
  22.9 0.0 copy-done
  22.9 0.5 %copy.15 = s32[1,1,128]{2,1,0:T(1,128)} copy(s32[1,1,128]{2,1,0:T(1,128)S(1)} %copy-done) | data formatting | bytes 1024
Async XLA Ops:
  21.3 1.6 %copy-start = (s32[1,1,128]{2,1,0:T(1,128)S(1)}, s32[1,1,128]{2,1,0:T(1,128)}, u32[]{:S(2)}) copy-start(s32[1,1,128]{2,1,0:T(1,128)} %get-tuple-element.5) | copy-start | bytes 1540
where the time goes:
time: 23.6 us; the launch traced here: 23.4 us
  Pallas kernels  20.1 us (85%)
  local copies, waits for them, and re-layouts  2.08 us (9%)
  between operations  1.3 us (6%)
    pallas_call x1, Pallas kernels, on_device(): pl.pallas_call(functools.partial(kernel, n_tm, n_sec, reach, cap), out_sh...  20.1 us
    unnamed x4, local copies, waits for them, and re-layouts  2.08 us

commit v1 on v0

--- a/solution.py
+++ b/solution.py
@@ -44,6 +44,7 @@
     ids_v,
     count_v,
     user_v,
+    hid,
     acc,
     cnt_send,
     cnt_recv,
@@ -53,6 +54,8 @@
     rows_recv,
     users_send,
     users_recv,
+    staged_rows,
+    staged_users,
     small_sem,
     ev_sem,
     w1_sem,
@@ -65,6 +68,7 @@
     rows_rs,
     users_ss,
     users_rs,
+    out_sem,
 ):
     t = lax.axis_index("tm")
     u = lax.axis_index("user")
@@ -74,6 +78,9 @@
     held = (reach + 1) * sess
     step = min(256, hidden)
     parts = hidden // step
+    padded = rows_send.shape[1]
+    direct = padded == cap
+    slots = n_sec * cap
 
     def load(src, dst, sem):
         copy = pltpu.make_async_copy(src, dst, sem)
@@ -93,10 +100,10 @@
             )
         )
     ]
-    w1_load, w2_load = [], []
+    w2_load = []
     for i in range(parts):
         cols = pl.ds(i * step, step)
-        w1_load.append(load(w_first.at[:, cols], w1_v.at[:, cols], w1_sem.at[i]))
+        load(w_first.at[:, cols], w1_v.at[:, cols], w1_sem.at[i])
         if i == 0:
             ev_load = load(events.at[0], ev_v, ev_sem)
     for i in range(parts):
@@ -137,29 +144,47 @@
             device_id_type=MESH,
         )
 
-    def routed_copy(k, send, recv, ss, rs):
+    def rows_copy(k):
         v = lax.rem(u + k, n_sec)
         return pltpu.make_async_remote_copy(
-            src_ref=send.at[v],
-            dst_ref=recv.at[u],
-            send_sem=ss.at[k - 1],
-            recv_sem=rs.at[k - 1],
+            src_ref=rows_send.at[v],
+            dst_ref=landing(),
+            send_sem=rows_ss.at[k - 1],
+            recv_sem=rows_rs.at[k - 1],
             device_id={"user": v},
             device_id_type=MESH,
         )
 
-    def rows_copy(k):
-        return routed_copy(k, rows_send, rows_recv, rows_ss, rows_rs)
+    def landing():
+        if direct:
+            return out_rows.at[0, 0, pl.ds(pl.multiple_of(u * cap, cap), cap)]
+        return rows_recv.at[u]
 
     def users_copy(k):
-        return routed_copy(k, users_send, users_recv, users_ss, users_rs)
+        v = lax.rem(u + k, n_sec)
+        return pltpu.make_async_remote_copy(
+            src_ref=users_send.at[v],
+            dst_ref=users_recv.at[u],
+            send_sem=users_ss.at[k - 1],
+            recv_sem=users_rs.at[k - 1],
+            device_id={"user": v},
+            device_id_type=MESH,
+        )
 
     c_one = math.sqrt(2.0 / math.pi)
     c_three = c_one * 0.044715
 
-    def activated(i):
-        cols = slice(i * step, (i + 1) * step)
-        tiles = []
+    def columns(i):
+        if isinstance(i, int):
+            return pl.ds(i * step, step)
+        return pl.ds(pl.multiple_of(i * step, step), step)
+
+    def activate(i):
+        cols = columns(i)
+        pltpu.make_async_copy(
+            w_first.at[:, cols], w1_v.at[:, cols], w1_sem.at[i]
+        ).wait()
+        slot = lax.rem(i, 2)
         for first in range(0, ev_rows, 256):
             x = jnp.dot(
                 ev_v[first : first + 256],
@@ -168,19 +193,19 @@
             )
             x = x + b1_v[:, cols]
             twice = x + x * jnp.tanh(x * (c_one + c_three * (x * x)))
-            tiles.append(twice.astype(BF16))
-        return jnp.concatenate(tiles, axis=0)
-
-    def second_product(i, active, rows):
-        cols = slice(i * step, (i + 1) * step)
+            hid[slot, first : first + 256] = twice.astype(BF16)
+
+    def second_product(i, rows):
+        active = hid[lax.rem(i, 2)]
         pooled = jnp.dot(assign[rows], active, preferred_element_type=F32)
-        return jnp.dot(pooled.astype(BF16), w2_v[cols, :], preferred_element_type=F32)
+        return jnp.dot(
+            pooled.astype(BF16), w2_v[columns(i), :], preferred_element_type=F32
+        )
 
     for copy in small:
         copy.wait()
-    w1_load[0].wait()
     ev_load.wait()
-    active = activated(0)
+    activate(0)
 
     ids = ids_v[...]
     local = ids - (t - reach) * sess
@@ -189,14 +214,17 @@
     belongs = jnp.where(local == iota((held, ev_rows), 0), 1.0, 0.0)
     assign = belongs.astype(BF16)
 
-    for copy in w1_load[1:] + w2_load:
+    for copy in w2_load:
         copy.wait()
     far = (reach + 1) // 2 * sess
-    total = second_product(0, active, slice(0, held))
-    for i in range(1, parts - 1):
-        total = total + second_product(i, activated(i), slice(0, held))
-    active = activated(parts - 1)
-    first_half = total[:far] + second_product(parts - 1, active, slice(0, far))
+    acc[...] = jnp.zeros_like(acc)
+
+    @pl.loop(1, parts)
+    def _(i):
+        activate(i)
+        acc[...] += second_product(i - 1, slice(0, held))
+
+    first_half = acc[:far] + second_product(parts - 1, slice(0, far))
     sums_send[: far // sess] = first_half.reshape(-1, sess, width).astype(BF16)
 
     pl.semaphore_wait(barrier, jnp.minimum(t, reach) + n_sec - 1)
@@ -208,12 +236,12 @@
 
     for d in range(reach, reach - far // sess, -1):
         send_sums(d)
-    rest = total[far:] + second_product(parts - 1, active, slice(far, held))
+    rest = acc[far:] + second_product(parts - 1, slice(far, held))
     near = rest[: held - far - sess]
     sums_send[far // sess :] = near.reshape(-1, sess, width).astype(BF16)
     for d in range(reach - far // sess, 0, -1):
         send_sums(d)
-    acc[...] = rest[held - far - sess :]
+    acc[:sess] = rest[held - far - sess :]
 
     totals = jnp.sum(belongs, axis=1, keepdims=True)
     diagonal = iota((sess, 128), 0) == iota((sess, 128), 1)
@@ -243,11 +271,9 @@
     rank_col = jnp.sum(
         jnp.where(square[1] < square[0], same, 0), axis=1, keepdims=True
     )
-    padded = rows_send.shape[1]
     place = jnp.where(
         sec_row * padded + rank_row == iota((n_sec * padded, sess), 0), 1.0, 0.0
     ).astype(BF16)
-    slots = n_sec * cap
     at = iota((sess, slots), 1) == rank_col + u * cap
     for v in range(n_sec):
         named = jnp.where(at & (sec_col == v), user_col + 1, 0)
@@ -272,23 +298,27 @@
     embedded = jnp.log(1.0 + count) * embed_v[...]
     for k in range(1, n_sec):
         users_copy(k).wait_recv()
-    out_users[0] = jnp.sum(users_recv[...], axis=0)[:1] - 1
+    staged_users[...] = jnp.sum(users_recv[...], axis=0)[:1] - 1
+    users_out = load(staged_users, out_users.at[0], out_sem.at[0])
 
     for d in range(1, reach + 1):
 
         @pl.when(t + d < n_tm)
         def _(d=d):
             sums_copy(d).wait_recv()
-            acc[...] += sums_recv[d - 1].astype(F32)
-
-    mixed = acc[...] * share + embedded
+            acc[:sess] += sums_recv[d - 1].astype(F32)
+
+    mixed = acc[:sess] * share + embedded
     mean = jnp.mean(mixed * mixed, axis=1, keepdims=True)
     rows = (mixed * lax.rsqrt(mean + 1e-06) * gain_v[...]).astype(BF16)
     outgoing = jnp.dot(place, rows, preferred_element_type=F32).astype(BF16)
     rows_send[...] = outgoing.reshape(n_sec, padded, width)
     for k in range(1, n_sec):
         rows_copy(k).start()
-    rows_recv[u] = rows_send[u]
+    if direct:
+        own = load(rows_send.at[u], landing(), out_sem.at[1])
+    else:
+        rows_recv[u] = rows_send[u]
 
     for d in range(1, reach + 1):
 
@@ -302,11 +332,29 @@
         rows_copy(k).wait_send()
     for k in range(1, n_sec):
         rows_copy(k).wait_recv()
-    if padded == cap:
-        out_rows[0, 0] = rows_recv[...].reshape(slots, width)
+    if direct:
+        own.wait()
     else:
         whole = rows_recv[...].astype(F32)[:, :cap]
-        out_rows[0, 0] = whole.reshape(slots, width).astype(BF16)
+        staged_rows[...] = whole.reshape(slots, width).astype(BF16)
+        load(staged_rows, out_rows.at[0, 0], out_sem.at[1]).wait()
+    users_out.wait()
+
+
+def hand_over(rows_in, users_in, rows_out, users_out, sem):
+    slots = rows_in.shape[2]
+    pieces = 4 if slots % 64 == 0 else 1
+    size = slots // pieces
+    copies = [pltpu.make_async_copy(users_in, users_out, sem.at[pieces])]
+    for i in range(pieces):
+        piece = (0, 0, pl.ds(i * size, size))
+        copies.append(
+            pltpu.make_async_copy(rows_in.at[piece], rows_out.at[piece], sem.at[i])
+        )
+    for copy in copies:
+        copy.start()
+    for copy in copies:
+        copy.wait()
 
 
 def on_device(
@@ -331,16 +379,16 @@
     slots = n_sec * cap
     parts = hidden // min(256, hidden)
     dma = pltpu.SemaphoreType.DMA
-    vmem = pl.BlockSpec(memory_space=pltpu.VMEM)
     hbm = pl.BlockSpec(memory_space=pl.ANY)
-    return pl.pallas_call(
+    out_shape = (
+        jax.ShapeDtypeStruct((1, 1, slots, width), BF16),
+        jax.ShapeDtypeStruct((1, 1, slots), I32),
+    )
+    routed = pl.pallas_call(
         functools.partial(kernel, n_tm, n_sec, reach, cap),
-        out_shape=(
-            jax.ShapeDtypeStruct((1, 1, slots, width), BF16),
-            jax.ShapeDtypeStruct((1, 1, slots), I32),
-        ),
+        out_shape=out_shape,
         in_specs=[hbm] * 9,
-        out_specs=(vmem, vmem),
+        out_specs=(hbm, hbm),
         scratch_shapes=[
             pltpu.VMEM((ev_rows, width), BF16),
             pltpu.VMEM((width, hidden), BF16),
@@ -351,7 +399,8 @@
             pltpu.VMEM((1, ev_rows), I32),
             pltpu.VMEM((1, 1), I32),
             pltpu.VMEM((1, sess), I32),
-            pltpu.VMEM((sess, width), F32),
+            pltpu.VMEM((2, ev_rows, hidden // parts), BF16),
+            pltpu.VMEM(((reach + 1) * sess, width), F32),
             pltpu.VMEM((reach + 1, 8, 128), F32),
             pltpu.VMEM((reach, 8, 128), F32),
             pltpu.VMEM((reach, sess, width), BF16),
@@ -360,6 +409,8 @@
             pltpu.VMEM((n_sec, padded, width), BF16),
             pltpu.VMEM((n_sec, 8, slots), I32),
             pltpu.VMEM((n_sec, 8, slots), I32),
+            pltpu.VMEM((slots, width), BF16),
+            pltpu.VMEM((1, slots), I32),
             dma((6,)),
             dma,
             dma((parts,)),
@@ -372,6 +423,7 @@
             dma((n_sec - 1,)),
             dma((n_sec - 1,)),
             dma((n_sec - 1,)),
+            dma((2,)),
         ],
         compiler_params=pltpu.CompilerParams(
             collective_id=0, has_side_effects=True, vmem_limit_bytes=VMEM_BYTES
@@ -388,6 +440,15 @@
         event_count,
         session_user,
     )
+    return pl.pallas_call(
+        hand_over,
+        out_shape=out_shape,
+        in_specs=[hbm] * 2,
+        out_specs=(hbm, hbm),
+        scratch_shapes=[dma((5,))],
+        compiler_params=pltpu.CompilerParams(vmem_limit_bytes=VMEM_BYTES),
+        name="hand_over",
+    )(*routed)
 
 
 def solution(mesh):

time: 23.6 us -> 27 us (1.14)
  Pallas kernels: 20.1 us -> 25.5 us
  local copies, waits for them, and re-layouts: 2.08 us -> 0 us
    pallas_call x0 -> x1, Pallas kernels: none -> 5.13 us  [on_device(): pl.pallas_call(hand_over, out_shape=out_shape, in_specs=[hbm] * 2, out_sp...]
    unnamed x4 -> x0, local copies, waits for them, and re-layouts: 2.08 us -> none
    pallas_call x1, Pallas kernels: 20.1 us -> 20.4 us  [on_device(): pl.pallas_call(functools.partial(kernel, n_tm, n_sec, reach, cap), out_sh...]
where the time goes in v1:
time: 27 us; the launch traced here: 26.8 us
  Pallas kernels  25.5 us (94%)
  between operations  1.29 us (5%)
    pallas_call x1, Pallas kernels, on_device(): pl.pallas_call(functools.partial(kernel, n_tm, n_sec, reach, cap), out_sh...  20.4 us
    pallas_call x1, Pallas kernels, on_device(): pl.pallas_call(hand_over, out_shape=out_shape, in_specs=[hbm] * 2, out_sp...  5.13 us

profile of v1, /device:TPU:2, one launch (start us, length us, event | category | flops | bytes accessed | tf_op | source)
XLA Modules:
  0.0 26.8 jit_solution(1094352099592989097)
XLA Ops:
  1.3 20.4 %pool_and_route.1 = (bf16[1,1,128,512]{3,2,1,0:T(8,128)(2,1)}, s32[1,1,128]{2,1,0:T(1,128)}) custom-call(bf16[1,1024,512]{2,1,0:T(8,128)(2,1)} %events.1, bf16[512,1024]{1,0:T(8,128)(2,1)} %w_first.1, bf16[1024,512]{1,0:T(8,128)(2,1)} %w_second.1, f32[1,1024]{1,0:T(1,128)} %bitcast.3, f32[1,512]{1,0:T(1,128)} %bitcast.4, f32[1,512]{1,0:T(1,128)} %bitcast.5, ...), custom_call_target="tpu_custom_call" | custom-call | tf_op jit(solution)/shard_map/pool_and_route/pallas_call | solution.py:387
  21.7 5.1 %hand_over.1 = (bf16[1,1,128,512]{3,2,1,0:T(8,128)(2,1)}, s32[1,1,128]{2,1,0:T(1,128)}) custom-call(bf16[1,1,128,512]{3,2,1,0:T(8,128)(2,1)} %get-tuple-element.4.rows_in, s32[1,1,128]{2,1,0:T(1,128)} %get-tuple-element.5.users_in), custom_call_target="tpu_custom_call" | custom-call | tf_op jit(solution)/shard_map/hand_over/pallas_call | solution.py:443

commit v2 on v0

--- a/solution.py
+++ b/solution.py
@@ -12,7 +12,7 @@
 BF16 = jnp.bfloat16
 F32 = jnp.float32
 I32 = jnp.int32
-VMEM_BYTES = 63 << 20
+VMEM_BYTES = 48 << 20
 
 
 def iota(shape, axis):
@@ -336,8 +336,8 @@
     return pl.pallas_call(
         functools.partial(kernel, n_tm, n_sec, reach, cap),
         out_shape=(
-            jax.ShapeDtypeStruct((1, 1, slots, width), BF16),
-            jax.ShapeDtypeStruct((1, 1, slots), I32),
+            pltpu.VMEM((1, 1, slots, width), BF16),
+            pltpu.VMEM((1, 1, slots), I32),
         ),
         in_specs=[hbm] * 9,
         out_specs=(vmem, vmem),
@@ -378,15 +378,22 @@
         ),
         name="pool_and_route",
     )(
-        events,
-        w_first,
-        w_second,
-        b_first.reshape(1, hidden),
-        count_embed.reshape(1, width),
-        norm_gain.reshape(1, width),
-        event_session,
-        event_count,
-        session_user,
+        *(
+            operand
+            if operand.size == 1
+            else pltpu.with_memory_space_constraint(operand, pltpu.HBM)
+            for operand in (
+                events,
+                w_first,
+                w_second,
+                b_first.reshape(1, hidden),
+                count_embed.reshape(1, width),
+                norm_gain.reshape(1, width),
+                event_session,
+                event_count,
+                session_user,
+            )
+        )
     )
 
 

time: 23.6 us -> 22.1 us (0.936)
  local copies, waits for them, and re-layouts: 2.08 us -> 1.17 us
  Pallas kernels: 20.1 us -> 19.4 us
    unnamed x4 -> x2, local copies, waits for them, and re-layouts: 2.08 us -> 1.17 us
    pallas_call x1, Pallas kernels: 20.1 us -> 19.4 us  [on_device(): pl.pallas_call(functools.partial(kernel, n_tm, n_sec, reach, cap), out_sh...]
where the time goes in v2:
time: 22.1 us; the launch traced here: 21.9 us
  Pallas kernels  19.4 us (88%)
  between operations  1.29 us (6%)
  local copies, waits for them, and re-layouts  1.17 us (5%)
    pallas_call x1, Pallas kernels, on_device(): pl.pallas_call(functools.partial(kernel, n_tm, n_sec, reach, cap), out_sh...  19.4 us
    unnamed x2, local copies, waits for them, and re-layouts  1.17 us

profile of v2, /device:TPU:2, one launch (start us, length us, event | category | flops | bytes accessed | tf_op | source)
XLA Modules:
  0.0 21.9 jit_solution(7449971722295041170)
XLA Ops:
  1.3 19.4 %pool_and_route.1 = (bf16[1,1,128,512]{3,2,1,0:T(8,128)(2,1)S(1)}, s32[1,1,128]{2,1,0:T(1,128)S(1)}) custom-call(bf16[1,1024,512]{2,1,0:T(8,128)(2,1)} %events.1, bf16[512,1024]{1,0:T(8,128)(2,1)} %w_first.1, bf16[1024,512]{1,0:T(8,128)(2,1)} %w_second.1, f32[1,1024]{1,0:T(1,128)} %bitcast.3, f32[1,512]{1,0:T(1,128)} %bitcast.4, f32[1,512]{1,0:T(1,128)} %bitcast.5, ...), custom_call_target="tpu_custom_call" | custom-call | tf_op jit(solution)/shard_map/pool_and_route/pallas_call | solution.py:336
  20.7 0.7 %copy.13 = bf16[1,1,128,512]{3,2,1,0:T(8,128)(2,1)} copy(bf16[1,1,128,512]{3,2,1,0:T(8,128)(2,1)S(1)} %get-tuple-element.2) | data formatting | bytes 262144
  21.4 0.5 %copy.14 = s32[1,1,128]{2,1,0:T(1,128)} copy(s32[1,1,128]{2,1,0:T(1,128)S(1)} %get-tuple-element.3) | data formatting | bytes 1024

commit v3 on v2

--- a/solution.py
+++ b/solution.py
@@ -74,6 +74,9 @@
     held = (reach + 1) * sess
     step = min(256, hidden)
     parts = hidden // step
+    padded = rows_send.shape[1]
+    direct = padded == cap
+    slots = n_sec * cap
 
     def load(src, dst, sem):
         copy = pltpu.make_async_copy(src, dst, sem)
@@ -137,39 +140,42 @@
             device_id_type=MESH,
         )
 
-    def routed_copy(k, send, recv, ss, rs):
+    def landing():
+        if direct:
+            return out_rows.at[0, 0, pl.ds(pl.multiple_of(u * cap, cap), cap)]
+        return rows_recv.at[u]
+
+    def rows_copy(k):
         v = lax.rem(u + k, n_sec)
         return pltpu.make_async_remote_copy(
-            src_ref=send.at[v],
-            dst_ref=recv.at[u],
-            send_sem=ss.at[k - 1],
-            recv_sem=rs.at[k - 1],
+            src_ref=rows_send.at[v],
+            dst_ref=landing(),
+            send_sem=rows_ss.at[k - 1],
+            recv_sem=rows_rs.at[k - 1],
             device_id={"user": v},
             device_id_type=MESH,
         )
 
-    def rows_copy(k):
-        return routed_copy(k, rows_send, rows_recv, rows_ss, rows_rs)
-
     def users_copy(k):
-        return routed_copy(k, users_send, users_recv, users_ss, users_rs)
+        v = lax.rem(u + k, n_sec)
+        return pltpu.make_async_remote_copy(
+            src_ref=users_send.at[v],
+            dst_ref=users_recv.at[u],
+            send_sem=users_ss.at[k - 1],
+            recv_sem=users_rs.at[k - 1],
+            device_id={"user": v},
+            device_id_type=MESH,
+        )
 
     c_one = math.sqrt(2.0 / math.pi)
     c_three = c_one * 0.044715
 
     def activated(i):
         cols = slice(i * step, (i + 1) * step)
-        tiles = []
-        for first in range(0, ev_rows, 256):
-            x = jnp.dot(
-                ev_v[first : first + 256],
-                w1_v[:, cols],
-                preferred_element_type=F32,
-            )
-            x = x + b1_v[:, cols]
-            twice = x + x * jnp.tanh(x * (c_one + c_three * (x * x)))
-            tiles.append(twice.astype(BF16))
-        return jnp.concatenate(tiles, axis=0)
+        x = jnp.dot(ev_v[...], w1_v[:, cols], preferred_element_type=F32)
+        x = x + b1_v[:, cols]
+        twice = x + x * jnp.tanh(x * (c_one + c_three * (x * x)))
+        return twice.astype(BF16)
 
     def second_product(i, active, rows):
         cols = slice(i * step, (i + 1) * step)
@@ -243,11 +249,9 @@
     rank_col = jnp.sum(
         jnp.where(square[1] < square[0], same, 0), axis=1, keepdims=True
     )
-    padded = rows_send.shape[1]
     place = jnp.where(
         sec_row * padded + rank_row == iota((n_sec * padded, sess), 0), 1.0, 0.0
     ).astype(BF16)
-    slots = n_sec * cap
     at = iota((sess, slots), 1) == rank_col + u * cap
     for v in range(n_sec):
         named = jnp.where(at & (sec_col == v), user_col + 1, 0)
@@ -288,7 +292,7 @@
     rows_send[...] = outgoing.reshape(n_sec, padded, width)
     for k in range(1, n_sec):
         rows_copy(k).start()
-    rows_recv[u] = rows_send[u]
+    landing()[...] = rows_send[u]
 
     for d in range(1, reach + 1):
 
@@ -302,9 +306,7 @@
         rows_copy(k).wait_send()
     for k in range(1, n_sec):
         rows_copy(k).wait_recv()
-    if padded == cap:
-        out_rows[0, 0] = rows_recv[...].reshape(slots, width)
-    else:
+    if not direct:
         whole = rows_recv[...].astype(F32)[:, :cap]
         out_rows[0, 0] = whole.reshape(slots, width).astype(BF16)
 

time: 22.1 us -> 23 us (1.041)
  Pallas kernels: 19.4 us -> 20.3 us
    pallas_call x1, Pallas kernels: 19.4 us -> 20.3 us  [on_device(): pl.pallas_call(functools.partial(kernel, n_tm, n_sec, reach, cap), out_sh...]
where the time goes in v3:
time: 23 us; the launch traced here: 22.8 us
  Pallas kernels  20.3 us (88%)
  between operations  1.29 us (6%)
  local copies, waits for them, and re-layouts  1.17 us (5%)
    pallas_call x1, Pallas kernels, on_device(): pl.pallas_call(functools.partial(kernel, n_tm, n_sec, reach, cap), out_sh...  20.3 us
    unnamed x2, local copies, waits for them, and re-layouts  1.17 us

profile of v3, /device:TPU:2, one launch (start us, length us, event | category | flops | bytes accessed | tf_op | source)
XLA Modules:
  0.0 22.8 jit_solution(13005066605843090886)
XLA Ops:
  1.3 20.3 %pool_and_route.1 = (bf16[1,1,128,512]{3,2,1,0:T(8,128)(2,1)S(1)}, s32[1,1,128]{2,1,0:T(1,128)S(1)}) custom-call(bf16[1,1024,512]{2,1,0:T(8,128)(2,1)} %events.1, bf16[512,1024]{1,0:T(8,128)(2,1)} %w_first.1, bf16[1024,512]{1,0:T(8,128)(2,1)} %w_second.1, f32[1,1024]{1,0:T(1,128)} %bitcast.3, f32[1,512]{1,0:T(1,128)} %bitcast.4, f32[1,512]{1,0:T(1,128)} %bitcast.5, ...), custom_call_target="tpu_custom_call" | custom-call | tf_op jit(solution)/shard_map/pool_and_route/pallas_call | solution.py:338
  21.6 0.7 %copy.13 = bf16[1,1,128,512]{3,2,1,0:T(8,128)(2,1)} copy(bf16[1,1,128,512]{3,2,1,0:T(8,128)(2,1)S(1)} %get-tuple-element.2) | data formatting | bytes 262144
  22.3 0.5 %copy.14 = s32[1,1,128]{2,1,0:T(1,128)} copy(s32[1,1,128]{2,1,0:T(1,128)S(1)} %get-tuple-element.3) | data formatting | bytes 1024

commit v4 on v2

--- a/solution.py
+++ b/solution.py
@@ -160,9 +160,9 @@
     def activated(i):
         cols = slice(i * step, (i + 1) * step)
         tiles = []
-        for first in range(0, ev_rows, 256):
+        for first in range(0, ev_rows, 128):
             x = jnp.dot(
-                ev_v[first : first + 256],
+                ev_v[first : first + 128],
                 w1_v[:, cols],
                 preferred_element_type=F32,
             )

time: 22.1 us -> 22.2 us (level)
  no operation moved by 1% of the time
where the time goes in v4:
time: 22.2 us; the launch traced here: 22 us
  Pallas kernels  19.6 us (88%)
  between operations  1.29 us (6%)
  local copies, waits for them, and re-layouts  1.17 us (5%)
    pallas_call x1, Pallas kernels, on_device(): pl.pallas_call(functools.partial(kernel, n_tm, n_sec, reach, cap), out_sh...  19.6 us
    unnamed x2, local copies, waits for them, and re-layouts  1.17 us

profile of v4, /device:TPU:2, one launch (start us, length us, event | category | flops | bytes accessed | tf_op | source)
XLA Modules:
  0.0 22.0 jit_solution(15729403383307059987)
XLA Ops:
  1.3 19.6 %pool_and_route.1 = (bf16[1,1,128,512]{3,2,1,0:T(8,128)(2,1)S(1)}, s32[1,1,128]{2,1,0:T(1,128)S(1)}) custom-call(bf16[1,1024,512]{2,1,0:T(8,128)(2,1)} %events.1, bf16[512,1024]{1,0:T(8,128)(2,1)} %w_first.1, bf16[1024,512]{1,0:T(8,128)(2,1)} %w_second.1, f32[1,1024]{1,0:T(1,128)} %bitcast.3, f32[1,512]{1,0:T(1,128)} %bitcast.4, f32[1,512]{1,0:T(1,128)} %bitcast.5, ...), custom_call_target="tpu_custom_call" | custom-call | tf_op jit(solution)/shard_map/pool_and_route/pallas_call | solution.py:336
  20.8 0.7 %copy.13 = bf16[1,1,128,512]{3,2,1,0:T(8,128)(2,1)} copy(bf16[1,1,128,512]{3,2,1,0:T(8,128)(2,1)S(1)} %get-tuple-element.2) | data formatting | bytes 262144
  21.5 0.5 %copy.14 = s32[1,1,128]{2,1,0:T(1,128)} copy(s32[1,1,128]{2,1,0:T(1,128)S(1)} %get-tuple-element.3) | data formatting | bytes 1024
